TPU v7x, 512 devices: a whole 4x8x8 slice. The times are simulated.
512 devices in a mesh: rep: 8 (over z_hi, core), row: 8 (over z_lo, x), col: 8 (over y).
Axes of the slice: x: 4, y: 8, z: 8 (z_hi: 4, z_lo: 2; z = z_hi * 2 + z_lo), core: 2. Of those that a mesh axis runs over, the one named last changes fastest.
Arguments:
- inputs: bfloat16 [8, 128, 6144], P('rep', 'col', 'row'), may hold values from -6 to 6
- w_in: bfloat16 [6144, 24576], P('row', ('rep', 'col')), may hold values from -0.078125 to 0.078125
- w_out: bfloat16 [24576, 6144], P(('rep', 'col'), 'row'), may hold values from -0.0390625 to 0.0390625
- cotangent: bfloat16 [8, 128, 6144], P('rep', 'col', 'row'), may hold values from -3072 to 3072
- counts: int32 [8], replicated, may hold values from 0 to 4, as said below
Outputs:
- block_output: bfloat16 [8, 128, 6144], P('rep', 'col', 'row')
- input_grad: bfloat16 [8, 128, 6144], P('rep', 'col', 'row')
- w_in_grad: float32 [6144, 24576], P('row', ('rep', 'col'))
- w_out_grad: float32 [24576, 6144], P(('rep', 'col'), 'row')
Inputs may be any that keep to these rules, and one draw needn't show every extreme that they name: Replica r completed its first counts[r] micro-batches; at least one replica completed all 4.
All inputs are finite; a program needn't handle non-finite values.
Results may differ from a plain program's by a relative error of at most 0.015.
Values may be sent and summed in bfloat16 or wider, within the bound.
No kernel may reach another device: no remote copies, remote signals or barrier semaphores. Data moves between devices by JAX's collectives and lax.ppermute only.
A program may use at most 64 MiB of HBM per device.

v0:
```python
import jax
import jax.numpy as jnp
from jax import lax
from jax.sharding import PartitionSpec as P

MBT = 32
root_coef = 0.7978845608028654
cubic_coef = 0.044715


def in_one_piece(arrays, axis, dim, along):
    both = jnp.concatenate(arrays, axis=along)
    result, at, finished = (lax.all_gather(both, axis, axis=dim, tiled=True), 0, [])
    for a in arrays:
        finished.append(lax.slice_in_dim(result, at, at + a.shape[along], axis=along))
        at += a.shape[along]
    return tuple(finished)


def split_up(value, dim, size):
    dims = value.shape
    pieces = value.reshape(*dims[:dim], size, dims[dim] // size, *dims[dim + 1 :])
    return jnp.moveaxis(pieces, dim, 0)


def summed_on_arrival(value, axis, dim):
    size = lax.axis_size(axis)
    pieces = lax.all_to_all(split_up(value, dim, size), axis, 0, 0, tiled=True)
    return jnp.sum(pieces.astype(jnp.float32), axis=0)


def sent_to_all(value, axis):
    size = lax.axis_size(axis)
    return lax.all_to_all(
        jnp.broadcast_to(value[None], (size, *value.shape)), axis, 0, 0, tiled=True
    )


def joined_along(pieces, dim):
    pieces = jnp.moveaxis(pieces, 0, dim)
    dims = pieces.shape
    return pieces.reshape(*dims[:dim], dims[dim] * dims[dim + 1], *dims[dim + 2 :])


def gathered_copies(value, axis, dim):
    pieces = sent_to_all(value, axis)
    return joined_along(pieces, dim)


def gelu_tanh(values):
    inner = root_coef * (values + cubic_coef * values * values * values)
    return 0.5 * values * (1.0 + jnp.tanh(inner))


def gelu_slope(values):
    inner = root_coef * (values + cubic_coef * values * values * values)
    tangent = jnp.tanh(inner)
    return 0.5 * (1.0 + tangent) + 0.5 * values * (1.0 - tangent * tangent) * root_coef * (
        1.0 + 3.0 * cubic_coef * values * values
    )


def right_product(left, right):
    return lax.dot_general(
        left, right, (((1,), (1,)), ((), ())), preferred_element_type=jnp.float32
    )


def first_product(left, right):
    return lax.dot_general(
        left, right, (((0,), (0,)), ((), ())), preferred_element_type=jnp.float32
    )


def body(inputs, w_in, w_out, cotangent, counts):
    rows_local = inputs.shape[1]
    width_local = inputs.shape[2]
    tokens_local = inputs.reshape(rows_local, width_local)
    replicas = lax.axis_size("rep")
    replica_index = lax.axis_index("rep")
    column_index = lax.axis_index("col")
    own_count = jnp.sum(jnp.where(jnp.arange(replicas) == replica_index, counts, 0))
    token_total = (MBT * jnp.sum(counts)).astype(jnp.float32)
    positions = column_index * rows_local + jnp.arange(rows_local, dtype=jnp.int32)
    kept_mask = (positions // MBT < own_count).astype(jnp.float32)
    scaled = (
        cotangent.reshape(rows_local, width_local).astype(jnp.float32)
        * kept_mask[:, None]
        / token_total
    ).astype(jnp.bfloat16)
    tokens_all, scaled_all = in_one_piece((tokens_local, scaled), "col", 0, 1)
    inner_cols = lax.all_gather(w_in, "rep", axis=1, tiled=True)
    outer_rows = lax.all_gather(w_out, "rep", axis=0, tiled=True)
    partial_hidden = jnp.dot(tokens_all, inner_cols, preferred_element_type=jnp.float32)
    hidden = summed_on_arrival(partial_hidden.astype(jnp.bfloat16), "row", 0)
    active_share = gelu_tanh(hidden).astype(jnp.bfloat16)
    activated = gathered_copies(active_share, "row", 0)
    output_terms = jnp.dot(activated, outer_rows, preferred_element_type=jnp.float32)
    output_local = summed_on_arrival(output_terms.astype(jnp.bfloat16), "col", 0)
    block_output = (tokens_local.astype(jnp.float32) + output_local).astype(jnp.bfloat16)
    slope_terms = right_product(scaled_all, outer_rows)
    slope_sum = summed_on_arrival(slope_terms.astype(jnp.bfloat16), "row", 0)
    grad_share = (slope_sum * gelu_slope(hidden)).astype(jnp.bfloat16)
    hidden_grad = gathered_copies(grad_share, "row", 0)
    back_terms = right_product(hidden_grad, inner_cols)
    back_local = summed_on_arrival(back_terms.astype(jnp.bfloat16), "col", 0)
    input_grad = (scaled.astype(jnp.float32) + back_local).astype(jnp.bfloat16)
    token_reps, scaled_reps = in_one_piece((tokens_all, scaled_all), "rep", 0, 1)
    hidden_reps, active_reps = (
        lax.all_to_all(hidden_grad, "rep", split_axis=1, concat_axis=0, tiled=True),
        lax.all_to_all(activated, "rep", split_axis=1, concat_axis=0, tiled=True),
    )
    w_in_grad = first_product(token_reps, hidden_reps)
    w_out_grad = first_product(active_reps, scaled_reps)
    return (
        block_output.reshape(1, rows_local, width_local),
        input_grad.reshape(1, rows_local, width_local),
        w_in_grad,
        w_out_grad,
    )


def solution(mesh):
    placed = (
        P("rep", "col", "row"),
        P("row", ("rep", "col")),
        P(("rep", "col"), "row"),
        P("rep", "col", "row"),
        P(),
    )
    return jax.shard_map(
        body,
        mesh=mesh,
        in_specs=placed,
        out_specs=(
            P("rep", "col", "row"),
            P("rep", "col", "row"),
            P("row", ("rep", "col")),
            P(("rep", "col"), "row"),
        ),
        check_vma=False,
    )
```

profile of v0, /device:TPU:2, one launch (start us, length us, event | category | flops | bytes accessed | tf_op | source)
XLA Modules:
  0.0 305.8 jit_solution(1008410382800476033)
XLA Ops:
  8.7 1.3 fusion.20
  11.3 0.8 fusion.15
  12.1 0.7 pad_maximum_fusion
  12.8 26.6 %all_gather.12 = bf16[128,1536]{1,0:T(8,128)(2,1)S(1)} all-gather(bf16[16,1536]{1,0:T(8,128)(2,1)S(1)} %pad_maximum_fusion), channel_id=1, replica_groups=mesh['rep'=8,'row'=8,'col'=8] {'col'}, dimensions={0}, use_global_device_ids=true | all-gather | bytes 442368 | tf_op jit(solution)/shard_map/all_gather | solution.py:13
  39.4 35.9 %all-gather.6.cloned.1.call-done = bf16[3072,768]{1,0:T(8,128)(2,1)} async-done(((bf16[384,768]{1,0:T(8,128)(2,1)}), bf16[3072,768]{1,0:T(8,128)(2,1)}) %all-gather.6.cloned.1.call-update) | async-done | bytes 4718608 | tf_op jit(solution)/shard_map/all_gather | solution.py:93
  75.3 4.9 %convolution_convert_fusion = bf16[128,3072]{1,0:T(8,128)(2,1)} fusion(bf16[3072,768]{1,0:T(8,128)(2,1)} %all-gather.6.cloned.1.call-done, bf16[128,1536]{1,0:T(8,128)(2,1)S(1)} %all_gather.12), kind=kOutput, calls=%fused_computation | convolution fusion | flops 604372992 | bytes 5701632 | tf_op jit(solution)/shard_map/dot_general | solution.py:64
  80.2 4.8 %all-to-all-start.3 = ((bf16[8,16,3072]{2,1,0:T(8,128)(2,1)}), bf16[8,16,3072]{2,1,0:T(8,128)(2,1)S(1)}, u32[]{:S(2)}, u32[]{:S(2)}) async-start(bf16[8,16,3072]{2,1,0:T(8,128)(2,1)} %bitcast.6), calls=%async_computation.3 | async-start | bytes 1572864 | tf_op jit(solution)/shard_map/all_to_all | solution.py:28
  85.0 53.2 %all-gather.4.cloned.1.call-done = bf16[768,3072]{1,0:T(8,128)(2,1)} async-done(((bf16[768,384]{1,0:T(8,128)(2,1)}), bf16[768,3072]{1,0:T(8,128)(2,1)}) %all-gather.4.cloned.1.call-update) | async-done | bytes 4718608 | tf_op jit(solution)/shard_map/all_gather | solution.py:92
  138.2 4.1 %convolution_convert_fusion.1 = bf16[128,3072]{1,0:T(8,128)(2,1)} fusion(bf16[768,3072]{1,0:T(8,128)(2,1)} %all-gather.4.cloned.1.call-done, bf16[128,1536]{1,0:T(8,128)(2,1)S(1)} %all_gather.12), kind=kOutput, calls=%fused_computation.1 | convolution fusion | flops 604372992 | bytes 5701632 | tf_op jit(solution)/shard_map/dot_general | solution.py:94
  142.3 4.8 %all-to-all-start = ((bf16[8,16,3072]{2,1,0:T(8,128)(2,1)}), bf16[8,16,3072]{2,1,0:T(8,128)(2,1)S(1)}, u32[]{:S(2)}, u32[]{:S(2)}) async-start(bf16[8,16,3072]{2,1,0:T(8,128)(2,1)} %bitcast.2), calls=%async_computation | async-start | bytes 1572864 | tf_op jit(solution)/shard_map/all_to_all | solution.py:28
  147.2 11.1 %all-to-all-done = bf16[8,16,3072]{2,1,0:T(8,128)(2,1)S(1)} async-done(((bf16[8,16,3072]{2,1,0:T(8,128)(2,1)}), bf16[8,16,3072]{2,1,0:T(8,128)(2,1)S(1)}, u32[]{:S(2)}, u32[]{:S(2)}) %all-to-all-start) | async-done | bytes 786464 | tf_op jit(solution)/shard_map/all_to_all | solution.py:28
  158.6 1.0 broadcast_in_dim.9
  159.6 4.8 %all-to-all-start.1 = ((bf16[8,16,3072]{2,1,0:T(8,128)(2,1)}), bf16[8,16,3072]{2,1,0:T(8,128)(2,1)S(1)}, u32[]{:S(2)}, u32[]{:S(2)}) async-start(bf16[8,16,3072]{2,1,0:T(8,128)(2,1)} %broadcast_in_dim.9), calls=%async_computation.1 | async-start | bytes 1572864 | tf_op jit(solution)/shard_map/all_to_all | solution.py:34
  164.4 0.7 all-gather.8.cloned.1.call-update
  165.1 10.3 %all-to-all-done.1 = bf16[8,16,3072]{2,1,0:T(8,128)(2,1)S(1)} async-done(((bf16[8,16,3072]{2,1,0:T(8,128)(2,1)}), bf16[8,16,3072]{2,1,0:T(8,128)(2,1)S(1)}, u32[]{:S(2)}, u32[]{:S(2)}) %all-to-all-start.1) | async-done | bytes 786464 | tf_op jit(solution)/shard_map/all_to_all | solution.py:34
  175.4 1.0 broadcast_in_dim.10
  176.3 4.8 %all-to-all-start.4 = ((bf16[8,16,3072]{2,1,0:T(8,128)(2,1)}), bf16[8,16,3072]{2,1,0:T(8,128)(2,1)S(1)}, u32[]{:S(2)}, u32[]{:S(2)}) async-start(bf16[8,16,3072]{2,1,0:T(8,128)(2,1)} %broadcast_in_dim.10), calls=%async_computation.4 | async-start | bytes 1572864 | tf_op jit(solution)/shard_map/all_to_all | solution.py:34
  181.2 3.8 %convolution_convert_fusion.3 = bf16[128,768]{1,0:T(8,128)(2,1)} fusion(bf16[128,3072]{1,0:T(8,128)(2,1)S(1)} %bitcast.43, bf16[3072,768]{1,0:T(8,128)(2,1)} %all-gather.6.cloned.1.call-done), kind=kOutput, calls=%fused_computation.9 | convolution fusion | flops 604078080 | bytes 5701632 | tf_op jit(solution)/shard_map/dot_general | solution.py:98
  185.0 26.9 %all-to-all-done.4 = bf16[8,16,3072]{2,1,0:T(8,128)(2,1)S(1)} async-done(((bf16[8,16,3072]{2,1,0:T(8,128)(2,1)}), bf16[8,16,3072]{2,1,0:T(8,128)(2,1)S(1)}, u32[]{:S(2)}, u32[]{:S(2)}) %all-to-all-start.4) | async-done | bytes 786464 | tf_op jit(solution)/shard_map/all_to_all | solution.py:34
  211.9 6.9 %all-to-all-start.2 = ((bf16[8,16,768]{2,1,0:T(8,128)(2,1)}), bf16[8,16,768]{2,1,0:T(8,128)(2,1)S(1)}, u32[]{:S(2)}, u32[]{:S(2)}) async-start(bf16[8,16,768]{2,1,0:T(8,128)(2,1)} %bitcast.4), calls=%async_computation.2 | async-start | bytes 393216 | tf_op jit(solution)/shard_map/all_to_all | solution.py:28
  218.8 4.7 %convolution_convert_fusion.2 = bf16[128,768]{1,0:T(8,128)(2,1)} fusion(bf16[128,3072]{1,0:T(8,128)(2,1)S(1)} %bitcast.45, bf16[768,3072]{1,0:T(8,128)(2,1)} %all-gather.4.cloned.1.call-done), kind=kOutput, calls=%fused_computation.8 | convolution fusion | flops 604078080 | bytes 5701632 | tf_op jit(solution)/shard_map/dot_general | solution.py:64
  223.5 5.3 %all-to-all-done.2 = bf16[8,16,768]{2,1,0:T(8,128)(2,1)S(1)} async-done(((bf16[8,16,768]{2,1,0:T(8,128)(2,1)}), bf16[8,16,768]{2,1,0:T(8,128)(2,1)S(1)}, u32[]{:S(2)}, u32[]{:S(2)}) %all-to-all-start.2) | async-done | bytes 196640 | tf_op jit(solution)/shard_map/all_to_all | solution.py:28
  228.7 3.4 %all-to-all-start.5 = ((bf16[8,16,768]{2,1,0:T(8,128)(2,1)}), bf16[8,16,768]{2,1,0:T(8,128)(2,1)S(1)}, u32[]{:S(2)}, u32[]{:S(2)}) async-start(bf16[8,16,768]{2,1,0:T(8,128)(2,1)} %bitcast.8), calls=%async_computation.5 | async-start | bytes 393216 | tf_op jit(solution)/shard_map/all_to_all | solution.py:28
  232.3 1.0 copy.11
  233.3 8.6 %all-to-all-done.5 = bf16[8,16,768]{2,1,0:T(8,128)(2,1)S(1)} async-done(((bf16[8,16,768]{2,1,0:T(8,128)(2,1)}), bf16[8,16,768]{2,1,0:T(8,128)(2,1)S(1)}, u32[]{:S(2)}, u32[]{:S(2)}) %all-to-all-start.5) | async-done | bytes 196640 | tf_op jit(solution)/shard_map/all_to_all | solution.py:28
  241.8 3.5 %all-to-all-start.6 = ((bf16[128,8,384]{2,0,1:T(8,128)(2,1)}), bf16[128,8,384]{2,0,1:T(8,128)(2,1)S(1)}, u32[]{:S(2)}, u32[]{:S(2)}) async-start(bf16[128,8,384]{2,0,1:T(8,128)(2,1)} %copy.11), calls=%async_computation.6 | async-start | bytes 1572864 | tf_op jit(solution)/shard_map/all_to_all | solution.py:110
  245.5 1.0 copy.12
  246.5 22.3 %all-to-all-done.6 = bf16[128,8,384]{2,0,1:T(8,128)(2,1)S(1)} async-done(((bf16[128,8,384]{2,0,1:T(8,128)(2,1)}), bf16[128,8,384]{2,0,1:T(8,128)(2,1)S(1)}, u32[]{:S(2)}, u32[]{:S(2)}) %all-to-all-start.6) | async-done | bytes 786464 | tf_op jit(solution)/shard_map/all_to_all | solution.py:110
  268.8 3.5 %all-to-all-start.7 = ((bf16[128,8,384]{2,0,1:T(8,128)(2,1)}), bf16[128,8,384]{2,0,1:T(8,128)(2,1)S(1)}, u32[]{:S(2)}, u32[]{:S(2)}) async-start(bf16[128,8,384]{2,0,1:T(8,128)(2,1)} %copy.12), calls=%async_computation.7 | async-start | bytes 1572864 | tf_op jit(solution)/shard_map/all_to_all | solution.py:111
  273.8 3.4 %fusion.2 = f32[768,384]{1,0:T(8,128)} fusion(bf16[1024,384]{1,0:T(8,128)(2,1)S(1)} %bitcast.49, bf16[1024,1536]{1,0:T(8,128)(2,1)} %all-gather.8.cloned.1.call-done), kind=kOutput, calls=%fused_computation.4 | convolution fusion | flops 603979776 | bytes 3538944 | tf_op jit(solution)/shard_map/dot_general | solution.py:70
  277.2 18.9 %all-to-all-done.7 = bf16[128,8,384]{2,0,1:T(8,128)(2,1)S(1)} async-done(((bf16[128,8,384]{2,0,1:T(8,128)(2,1)}), bf16[128,8,384]{2,0,1:T(8,128)(2,1)S(1)}, u32[]{:S(2)}, u32[]{:S(2)}) %all-to-all-start.7) | async-done | bytes 786464 | tf_op jit(solution)/shard_map/all_to_all | solution.py:111
  296.1 3.2 %fusion = f32[384,768]{1,0:T(8,128)} fusion(bf16[1024,384]{1,0:T(8,128)(2,1)S(1)} %bitcast.50, bf16[1024,1536]{1,0:T(8,128)(2,1)} %all-gather.8.cloned.1.call-done), kind=kOutput, calls=%fused_computation.2 | convolution fusion | flops 603979776 | bytes 3538944 | tf_op jit(solution)/shard_map/dot_general | solution.py:70
  (23 shorter events, 4.1 us)
Async XLA Ops:
  7.2 68.2 %all-gather.6.cloned.1.call-start = ((), (), s32[]{:S(2)}) async-start(), calls=%async_computation.9 | async-start | bytes 5308416 | tf_op jit(solution)/shard_map/all_gather | solution.py:93
  7.9 130.3 %all-gather.4.cloned.1.call-start = ((), (), s32[]{:S(2)}) async-start(), calls=%async_computation.8 | async-start | bytes 5308416 | tf_op jit(solution)/shard_map/all_gather | solution.py:92
  39.4 98.8 %copy-start = (bf16[128,1536]{1,0:T(8,128)(2,1)}, bf16[128,1536]{1,0:T(8,128)(2,1)S(1)}, u32[]{:S(2)}) copy-start(bf16[128,1536]{1,0:T(8,128)(2,1)S(1)} %all_gather.12) | copy-start | bytes 1179652
  80.2 62.1 %all-to-all-start.3 = ((bf16[8,16,3072]{2,1,0:T(8,128)(2,1)}), bf16[8,16,3072]{2,1,0:T(8,128)(2,1)S(1)}, u32[]{:S(2)}, u32[]{:S(2)}) async-start(bf16[8,16,3072]{2,1,0:T(8,128)(2,1)} %bitcast.6), calls=%async_computation.3 | async-start | bytes 1572864 | tf_op jit(solution)/shard_map/all_to_all | solution.py:28
  142.3 16.1 %all-to-all-start = ((bf16[8,16,3072]{2,1,0:T(8,128)(2,1)}), bf16[8,16,3072]{2,1,0:T(8,128)(2,1)S(1)}, u32[]{:S(2)}, u32[]{:S(2)}) async-start(bf16[8,16,3072]{2,1,0:T(8,128)(2,1)} %bitcast.2), calls=%async_computation | async-start | bytes 1572864 | tf_op jit(solution)/shard_map/all_to_all | solution.py:28
  159.6 15.8 %all-to-all-start.1 = ((bf16[8,16,3072]{2,1,0:T(8,128)(2,1)}), bf16[8,16,3072]{2,1,0:T(8,128)(2,1)S(1)}, u32[]{:S(2)}, u32[]{:S(2)}) async-start(bf16[8,16,3072]{2,1,0:T(8,128)(2,1)} %broadcast_in_dim.9), calls=%async_computation.1 | async-start | bytes 1572864 | tf_op jit(solution)/shard_map/all_to_all | solution.py:34
  164.4 109.4 %all-gather.8.cloned.1.call-start = ((), (), s32[]{:S(2)}) async-start(), calls=%async_computation.10 | async-start | bytes 3538944 | tf_op jit(solution)/shard_map/all_gather | solution.py:13
  176.3 35.5 %all-to-all-start.4 = ((bf16[8,16,3072]{2,1,0:T(8,128)(2,1)}), bf16[8,16,3072]{2,1,0:T(8,128)(2,1)S(1)}, u32[]{:S(2)}, u32[]{:S(2)}) async-start(bf16[8,16,3072]{2,1,0:T(8,128)(2,1)} %broadcast_in_dim.10), calls=%async_computation.4 | async-start | bytes 1572864 | tf_op jit(solution)/shard_map/all_to_all | solution.py:34
  211.9 16.9 %all-to-all-start.2 = ((bf16[8,16,768]{2,1,0:T(8,128)(2,1)}), bf16[8,16,768]{2,1,0:T(8,128)(2,1)S(1)}, u32[]{:S(2)}, u32[]{:S(2)}) async-start(bf16[8,16,768]{2,1,0:T(8,128)(2,1)} %bitcast.4), calls=%async_computation.2 | async-start | bytes 393216 | tf_op jit(solution)/shard_map/all_to_all | solution.py:28
  228.7 13.1 %all-to-all-start.5 = ((bf16[8,16,768]{2,1,0:T(8,128)(2,1)}), bf16[8,16,768]{2,1,0:T(8,128)(2,1)S(1)}, u32[]{:S(2)}, u32[]{:S(2)}) async-start(bf16[8,16,768]{2,1,0:T(8,128)(2,1)} %bitcast.8), calls=%async_computation.5 | async-start | bytes 393216 | tf_op jit(solution)/shard_map/all_to_all | solution.py:28
  233.3 39.2 %copy-start.2 = (bf16[1,16,768]{2,1,0:T(8,128)(2,1)S(1)}, bf16[1,16,768]{2,1,0:T(8,128)(2,1)}, u32[]{:S(2)}) copy-start(bf16[1,16,768]{2,1,0:T(8,128)(2,1)} %param.5) | copy-start | bytes 73732
  233.3 39.8 %copy-start.1 = (bf16[1,16,768]{2,1,0:T(8,128)(2,1)S(1)}, bf16[1,16,768]{2,1,0:T(8,128)(2,1)}, u32[]{:S(2)}) copy-start(bf16[1,16,768]{2,1,0:T(8,128)(2,1)} %param.8) | copy-start | bytes 73732
  241.8 27.0 %all-to-all-start.6 = ((bf16[128,8,384]{2,0,1:T(8,128)(2,1)}), bf16[128,8,384]{2,0,1:T(8,128)(2,1)S(1)}, u32[]{:S(2)}, u32[]{:S(2)}) async-start(bf16[128,8,384]{2,0,1:T(8,128)(2,1)} %copy.11), calls=%async_computation.6 | async-start | bytes 1572864 | tf_op jit(solution)/shard_map/all_to_all | solution.py:110
  268.8 27.3 %all-to-all-start.7 = ((bf16[128,8,384]{2,0,1:T(8,128)(2,1)}), bf16[128,8,384]{2,0,1:T(8,128)(2,1)S(1)}, u32[]{:S(2)}, u32[]{:S(2)}) async-start(bf16[128,8,384]{2,0,1:T(8,128)(2,1)} %copy.12), calls=%async_computation.7 | async-start | bytes 1572864 | tf_op jit(solution)/shard_map/all_to_all | solution.py:111
Sparse Core Ops, SparseCore 0:
  10.1 65.1 all-gather.5
  77.5 60.7 all-gather.3
  167.3 52.0 all-gather.7
where the time goes:
time: 307 us; the launch traced here: 306 us
  waiting for transfers between devices  195 us (64%)
  starting transfers between devices  36.7 us (12%)
  blocking collectives  26.6 us (9%)
  matrix products  24.1 us (8%)
  between operations  14.5 us (5%)
  other arithmetic  5.26 us (2%)
  local copies, waits for them, and re-layouts  4.15 us (1%)
    all_gather x1, waiting for transfers between devices, body(): inner_cols = lax.all_gather(w_in, 'rep', axis=1, tiled=True)  53.2 us
    all_to_all x2, waiting for transfers between devices, sent_to_all(): lax.all_to_all(jnp.broadcast_to(value[None], (size, *value.shape)), axis,...  37.2 us
    all_gather x1, waiting for transfers between devices, body(): outer_rows = lax.all_gather(w_out, 'rep', axis=0, tiled=True)  35.9 us
    all_gather x1, blocking collectives, in_one_piece(): lax.all_gather(both, axis, axis=dim, tiled=True)  26.6 us
    all_to_all x4, waiting for transfers between devices, summed_on_arrival(): pieces = lax.all_to_all(split_up(value, dim, size), axis, 0, 0, tiled=True)  25 us
    all_to_all x1, waiting for transfers between devices, body(): lax.all_to_all(hidden_grad, 'rep', split_axis=1, concat_axis=0, tiled=True)  22.3 us
    all_to_all x4, starting transfers between devices, summed_on_arrival(): pieces = lax.all_to_all(split_up(value, dim, size), axis, 0, 0, tiled=True)  19.9 us
    all_to_all x1, waiting for transfers between devices, body(): lax.all_to_all(activated, 'rep', split_axis=1, concat_axis=0, tiled=True)  18.9 us
  transfers between devices with their start and end apart: 11, of which 9 were waited for; matrix products, arithmetic and copies ran while one was open for 10% of the time, Pallas kernels for 0%

commit v1 on v0

--- a/solution.py
+++ b/solution.py
@@ -89,7 +89,9 @@
         / token_total
     ).astype(jnp.bfloat16)
     tokens_all, scaled_all = in_one_piece((tokens_local, scaled), "col", 0, 1)
-    inner_cols = lax.all_gather(w_in, "rep", axis=1, tiled=True)
+    inner_cols = jnp.concatenate(
+        lax.all_to_all(jnp.stack([w_in] * lax.axis_size("rep")), "rep", 0, 0), axis=1
+    )
     outer_rows = lax.all_gather(w_out, "rep", axis=0, tiled=True)
     partial_hidden = jnp.dot(tokens_all, inner_cols, preferred_element_type=jnp.float32)
     hidden = summed_on_arrival(partial_hidden.astype(jnp.bfloat16), "row", 0)

time: 307 us -> 353 us (1.15)
  waiting for transfers between devices: 195 us -> 221 us
  starting transfers between devices: 36.7 us -> 54.4 us
  local copies, waits for them, and re-layouts: 4.15 us -> 7.99 us
    all_gather x1 -> x0, waiting for transfers between devices: 53.2 us -> none  [body(): inner_cols = lax.all_gather(w_in, 'rep', axis=1, tiled=True)]
    all_gather x1, waiting for transfers between devices: 35.9 us -> 80.2 us  [body(): outer_rows = lax.all_gather(w_out, 'rep', axis=0, tiled=True)]
    all_to_all x0 -> x1, waiting for transfers between devices: none -> 32.6 us  [body(): lax.all_to_all(jnp.stack([w_in] * lax.axis_size('rep')), 'rep', 0, 0)]
    all_to_all x0 -> x1, starting transfers between devices: none -> 10.4 us  [body(): lax.all_to_all(jnp.stack([w_in] * lax.axis_size('rep')), 'rep', 0, 0)]
    all_to_all x4, waiting for transfers between devices: 25 us -> 31.8 us  [summed_on_arrival(): pieces = lax.all_to_all(split_up(value, dim, size), axis, 0, 0, tiled=True)]
    all_to_all x4, starting transfers between devices: 19.9 us -> 24.2 us  [summed_on_arrival(): pieces = lax.all_to_all(split_up(value, dim, size), axis, 0, 0, tiled=True)]
    all_to_all x2, waiting for transfers between devices: 37.2 us -> 33.4 us  [sent_to_all(): lax.all_to_all(jnp.broadcast_to(value[None], (size, *value.shape)), axis,...]
  transfers between devices with their start and end apart: 11 -> 11, of which waited for: 9 -> 10; matrix products, arithmetic and copies ran while one was open for 10% -> 9% of each run, Pallas kernels for 0% -> 0%
where the time goes in v1:
time: 353 us; the launch traced here: 352 us
  waiting for transfers between devices  221 us (63%)
  starting transfers between devices  54.4 us (15%)
  blocking collectives  26.6 us (8%)
  matrix products  24.4 us (7%)
  between operations  14.8 us (4%)
  local copies, waits for them, and re-layouts  7.99 us (2%)
    all_gather x1, waiting for transfers between devices, body(): outer_rows = lax.all_gather(w_out, 'rep', axis=0, tiled=True)  80.2 us
    all_to_all x2, waiting for transfers between devices, sent_to_all(): lax.all_to_all(jnp.broadcast_to(value[None], (size, *value.shape)), axis,...  33.4 us
    all_to_all x1, waiting for transfers between devices, body(): lax.all_to_all(jnp.stack([w_in] * lax.axis_size('rep')), 'rep', 0, 0)  32.6 us
    all_to_all x4, waiting for transfers between devices, summed_on_arrival(): pieces = lax.all_to_all(split_up(value, dim, size), axis, 0, 0, tiled=True)  31.8 us
    all_gather x1, blocking collectives, in_one_piece(): lax.all_gather(both, axis, axis=dim, tiled=True)  26.6 us
    all_to_all x4, starting transfers between devices, summed_on_arrival(): pieces = lax.all_to_all(split_up(value, dim, size), axis, 0, 0, tiled=True)  24.2 us
    all_to_all x1, waiting for transfers between devices, body(): lax.all_to_all(hidden_grad, 'rep', split_axis=1, concat_axis=0, tiled=True)  22.9 us
    all_to_all x1, waiting for transfers between devices, body(): lax.all_to_all(activated, 'rep', split_axis=1, concat_axis=0, tiled=True)  18.5 us
  transfers between devices with their start and end apart: 11, of which 10 were waited for; matrix products, arithmetic and copies ran while one was open for 9% of the time, Pallas kernels for 0%

profile of v1, /device:TPU:2, one launch (start us, length us, event | category | flops | bytes accessed | tf_op | source)
XLA Modules:
  0.0 352.0 jit_solution(13270111245365748383)
XLA Ops:
  7.9 1.3 copy.13
  9.2 2.5 stack.2
  11.7 10.4 %all-to-all-start = ((bf16[8,768,384]{1,2,0:T(8,128)(2,1)}), bf16[8,768,384]{1,2,0:T(8,128)(2,1)}, u32[]{:S(2)}, u32[]{:S(2)}) async-start(bf16[8,768,384]{1,2,0:T(8,128)(2,1)} %stack.2), calls=%async_computation | async-start | bytes 9437184 | tf_op jit(solution)/shard_map/all_to_all | solution.py:93
  24.3 26.6 %all_gather.9 = bf16[128,1536]{1,0:T(8,128)(2,1)S(1)} all-gather(bf16[16,1536]{1,0:T(8,128)(2,1)S(1)} %pad_maximum_fusion), channel_id=1, replica_groups=mesh['rep'=8,'row'=8,'col'=8] {'col'}, dimensions={0}, use_global_device_ids=true | all-gather | bytes 442368 | tf_op jit(solution)/shard_map/all_gather | solution.py:13
  50.8 80.2 %all-gather.3.cloned.1.call-done = bf16[3072,768]{1,0:T(8,128)(2,1)} async-done(((bf16[384,768]{1,0:T(8,128)(2,1)}), bf16[3072,768]{1,0:T(8,128)(2,1)}) %all-gather.3.cloned.1.call-update) | async-done | bytes 4718608 | tf_op jit(solution)/shard_map/all_gather | solution.py:95
  131.1 4.9 %convolution_convert_fusion = bf16[128,3072]{1,0:T(8,128)(2,1)} fusion(bf16[3072,768]{1,0:T(8,128)(2,1)} %all-gather.3.cloned.1.call-done, bf16[128,1536]{1,0:T(8,128)(2,1)S(1)} %all_gather.9), kind=kOutput, calls=%fused_computation | convolution fusion | flops 604372992 | bytes 5701632 | tf_op jit(solution)/shard_map/dot_general | solution.py:64
  135.9 32.6 %all-to-all-done = bf16[8,768,384]{1,2,0:T(8,128)(2,1)} async-done(((bf16[8,768,384]{1,2,0:T(8,128)(2,1)}), bf16[8,768,384]{1,2,0:T(8,128)(2,1)}, u32[]{:S(2)}, u32[]{:S(2)}) %all-to-all-start) | async-done | bytes 4718624 | tf_op jit(solution)/shard_map/all_to_all | solution.py:93
  168.5 8.6 %all-to-all-start.4 = ((bf16[8,16,3072]{2,1,0:T(8,128)(2,1)}), bf16[8,16,3072]{2,1,0:T(8,128)(2,1)S(1)}, u32[]{:S(2)}, u32[]{:S(2)}) async-start(bf16[8,16,3072]{2,1,0:T(8,128)(2,1)} %bitcast.8), calls=%async_computation.4 | async-start | bytes 1572864 | tf_op jit(solution)/shard_map/all_to_all | solution.py:28
  177.0 4.8 %convolution_convert_fusion.1 = bf16[128,3072]{1,0:T(8,128)(2,1)} fusion(bf16[768,3072]{0,1:T(8,128)(2,1)} %bitcast.3, bf16[128,1536]{1,0:T(8,128)(2,1)S(1)} %all_gather.9), kind=kOutput, calls=%fused_computation.1 | convolution fusion | flops 604372992 | bytes 5701632 | tf_op jit(solution)/shard_map/dot_general | solution.py:96
  181.9 6.4 %all-to-all-done.4 = bf16[8,16,3072]{2,1,0:T(8,128)(2,1)S(1)} async-done(((bf16[8,16,3072]{2,1,0:T(8,128)(2,1)}), bf16[8,16,3072]{2,1,0:T(8,128)(2,1)S(1)}, u32[]{:S(2)}, u32[]{:S(2)}) %all-to-all-start.4) | async-done | bytes 786464 | tf_op jit(solution)/shard_map/all_to_all | solution.py:28
  188.3 4.8 %all-to-all-start.1 = ((bf16[8,16,3072]{2,1,0:T(8,128)(2,1)}), bf16[8,16,3072]{2,1,0:T(8,128)(2,1)S(1)}, u32[]{:S(2)}, u32[]{:S(2)}) async-start(bf16[8,16,3072]{2,1,0:T(8,128)(2,1)} %bitcast.4), calls=%async_computation.1 | async-start | bytes 1572864 | tf_op jit(solution)/shard_map/all_to_all | solution.py:28
  193.2 10.9 %all-to-all-done.1 = bf16[8,16,3072]{2,1,0:T(8,128)(2,1)S(1)} async-done(((bf16[8,16,3072]{2,1,0:T(8,128)(2,1)}), bf16[8,16,3072]{2,1,0:T(8,128)(2,1)S(1)}, u32[]{:S(2)}, u32[]{:S(2)}) %all-to-all-start.1) | async-done | bytes 786464 | tf_op jit(solution)/shard_map/all_to_all | solution.py:28
  204.3 1.0 broadcast_in_dim.9
  205.3 4.8 %all-to-all-start.2 = ((bf16[8,16,3072]{2,1,0:T(8,128)(2,1)}), bf16[8,16,3072]{2,1,0:T(8,128)(2,1)S(1)}, u32[]{:S(2)}, u32[]{:S(2)}) async-start(bf16[8,16,3072]{2,1,0:T(8,128)(2,1)} %broadcast_in_dim.9), calls=%async_computation.2 | async-start | bytes 1572864 | tf_op jit(solution)/shard_map/all_to_all | solution.py:34
  210.8 10.3 %all-to-all-done.2 = bf16[8,16,3072]{2,1,0:T(8,128)(2,1)S(1)} async-done(((bf16[8,16,3072]{2,1,0:T(8,128)(2,1)}), bf16[8,16,3072]{2,1,0:T(8,128)(2,1)S(1)}, u32[]{:S(2)}, u32[]{:S(2)}) %all-to-all-start.2) | async-done | bytes 786464 | tf_op jit(solution)/shard_map/all_to_all | solution.py:34
  221.1 1.0 broadcast_in_dim.10
  222.1 4.8 %all-to-all-start.5 = ((bf16[8,16,3072]{2,1,0:T(8,128)(2,1)}), bf16[8,16,3072]{2,1,0:T(8,128)(2,1)S(1)}, u32[]{:S(2)}, u32[]{:S(2)}) async-start(bf16[8,16,3072]{2,1,0:T(8,128)(2,1)} %broadcast_in_dim.10), calls=%async_computation.5 | async-start | bytes 1572864 | tf_op jit(solution)/shard_map/all_to_all | solution.py:34
  226.9 4.2 %convolution_convert_fusion.3 = bf16[128,768]{1,0:T(8,128)(2,1)} fusion(bf16[128,3072]{1,0:T(8,128)(2,1)S(1)} %bitcast.46, bf16[3072,768]{1,0:T(8,128)(2,1)} %all-gather.3.cloned.1.call-done), kind=kOutput, calls=%fused_computation.9 | convolution fusion | flops 604078080 | bytes 5701632 | tf_op jit(solution)/shard_map/dot_general | solution.py:100
  231.1 23.2 %all-to-all-done.5 = bf16[8,16,3072]{2,1,0:T(8,128)(2,1)S(1)} async-done(((bf16[8,16,3072]{2,1,0:T(8,128)(2,1)}), bf16[8,16,3072]{2,1,0:T(8,128)(2,1)S(1)}, u32[]{:S(2)}, u32[]{:S(2)}) %all-to-all-start.5) | async-done | bytes 786464 | tf_op jit(solution)/shard_map/all_to_all | solution.py:34
  254.2 7.4 %all-to-all-start.3 = ((bf16[8,16,768]{2,1,0:T(8,128)(2,1)}), bf16[8,16,768]{2,1,0:T(8,128)(2,1)S(1)}, u32[]{:S(2)}, u32[]{:S(2)}) async-start(bf16[8,16,768]{2,1,0:T(8,128)(2,1)} %bitcast.6), calls=%async_computation.3 | async-start | bytes 393216 | tf_op jit(solution)/shard_map/all_to_all | solution.py:28
  261.7 3.9 %convolution_convert_fusion.2 = bf16[128,768]{1,0:T(8,128)(2,1)} fusion(bf16[128,3072]{1,0:T(8,128)(2,1)S(1)} %bitcast.48, bf16[768,3072]{0,1:T(8,128)(2,1)} %bitcast.3), kind=kOutput, calls=%fused_computation.8 | convolution fusion | flops 604078080 | bytes 5701632 | tf_op jit(solution)/shard_map/dot_general | solution.py:64
  265.5 5.9 %all-to-all-done.3 = bf16[8,16,768]{2,1,0:T(8,128)(2,1)S(1)} async-done(((bf16[8,16,768]{2,1,0:T(8,128)(2,1)}), bf16[8,16,768]{2,1,0:T(8,128)(2,1)S(1)}, u32[]{:S(2)}, u32[]{:S(2)}) %all-to-all-start.3) | async-done | bytes 196640 | tf_op jit(solution)/shard_map/all_to_all | solution.py:28
  271.5 3.4 all-to-all-start.6
  275.0 1.0 copy.14
  276.0 8.6 %all-to-all-done.6 = bf16[8,16,768]{2,1,0:T(8,128)(2,1)S(1)} async-done(((bf16[8,16,768]{2,1,0:T(8,128)(2,1)}), bf16[8,16,768]{2,1,0:T(8,128)(2,1)S(1)}, u32[]{:S(2)}, u32[]{:S(2)}) %all-to-all-start.6) | async-done | bytes 196640 | tf_op jit(solution)/shard_map/all_to_all | solution.py:28
  284.5 6.5 %all-to-all-start.7 = ((bf16[128,8,384]{2,0,1:T(8,128)(2,1)}), bf16[128,8,384]{2,0,1:T(8,128)(2,1)S(1)}, u32[]{:S(2)}, u32[]{:S(2)}) async-start(bf16[128,8,384]{2,0,1:T(8,128)(2,1)} %copy.14), calls=%async_computation.7 | async-start | bytes 1572864 | tf_op jit(solution)/shard_map/all_to_all | solution.py:112
  291.2 1.0 copy.15
  292.2 22.9 %all-to-all-done.7 = bf16[128,8,384]{2,0,1:T(8,128)(2,1)S(1)} async-done(((bf16[128,8,384]{2,0,1:T(8,128)(2,1)}), bf16[128,8,384]{2,0,1:T(8,128)(2,1)S(1)}, u32[]{:S(2)}, u32[]{:S(2)}) %all-to-all-start.7) | async-done | bytes 786464 | tf_op jit(solution)/shard_map/all_to_all | solution.py:112
  315.1 3.5 %all-to-all-start.8 = ((bf16[128,8,384]{2,0,1:T(8,128)(2,1)}), bf16[128,8,384]{2,0,1:T(8,128)(2,1)S(1)}, u32[]{:S(2)}, u32[]{:S(2)}) async-start(bf16[128,8,384]{2,0,1:T(8,128)(2,1)} %copy.15), calls=%async_computation.8 | async-start | bytes 1572864 | tf_op jit(solution)/shard_map/all_to_all | solution.py:113
  320.0 3.4 fusion.2
  323.4 18.5 %all-to-all-done.8 = bf16[128,8,384]{2,0,1:T(8,128)(2,1)S(1)} async-done(((bf16[128,8,384]{2,0,1:T(8,128)(2,1)}), bf16[128,8,384]{2,0,1:T(8,128)(2,1)S(1)}, u32[]{:S(2)}, u32[]{:S(2)}) %all-to-all-start.8) | async-done | bytes 786464 | tf_op jit(solution)/shard_map/all_to_all | solution.py:113
  341.9 3.2 fusion
  (26 shorter events, 4.8 us)
Async XLA Ops:
  7.2 123.9 %all-gather.3.cloned.1.call-start = ((), (), s32[]{:S(2)}) async-start(), calls=%async_computation.9 | async-start | bytes 5308416 | tf_op jit(solution)/shard_map/all_gather | solution.py:95
  11.7 10.4 %copy-start.3 = (s32[8]{0:T(128)S(1)}, s32[8]{0:T(128)}, u32[]{:S(2)}) copy-start(s32[8]{0:T(128)} %param.9) | copy-start | bytes 100
  11.7 12.4 %copy-start.1 = (bf16[1,16,768]{2,1,0:T(8,128)(2,1)S(1)}, bf16[1,16,768]{2,1,0:T(8,128)(2,1)}, u32[]{:S(2)}) copy-start(bf16[1,16,768]{2,1,0:T(8,128)(2,1)} %param.8) | copy-start | bytes 73732
  11.7 12.5 %copy-start.2 = (bf16[1,16,768]{2,1,0:T(8,128)(2,1)S(1)}, bf16[1,16,768]{2,1,0:T(8,128)(2,1)}, u32[]{:S(2)}) copy-start(bf16[1,16,768]{2,1,0:T(8,128)(2,1)} %param.5) | copy-start | bytes 73732
  11.7 156.7 %all-to-all-start = ((bf16[8,768,384]{1,2,0:T(8,128)(2,1)}), bf16[8,768,384]{1,2,0:T(8,128)(2,1)}, u32[]{:S(2)}, u32[]{:S(2)}) async-start(bf16[8,768,384]{1,2,0:T(8,128)(2,1)} %stack.2), calls=%async_computation | async-start | bytes 9437184 | tf_op jit(solution)/shard_map/all_to_all | solution.py:93
  50.8 126.2 %copy-start = (bf16[128,1536]{1,0:T(8,128)(2,1)}, bf16[128,1536]{1,0:T(8,128)(2,1)S(1)}, u32[]{:S(2)}) copy-start(bf16[128,1536]{1,0:T(8,128)(2,1)S(1)} %all_gather.9) | copy-start | bytes 1179652
  168.5 19.8 %all-to-all-start.4 = ((bf16[8,16,3072]{2,1,0:T(8,128)(2,1)}), bf16[8,16,3072]{2,1,0:T(8,128)(2,1)S(1)}, u32[]{:S(2)}, u32[]{:S(2)}) async-start(bf16[8,16,3072]{2,1,0:T(8,128)(2,1)} %bitcast.8), calls=%async_computation.4 | async-start | bytes 1572864 | tf_op jit(solution)/shard_map/all_to_all | solution.py:28
  188.3 15.8 %all-to-all-start.1 = ((bf16[8,16,3072]{2,1,0:T(8,128)(2,1)}), bf16[8,16,3072]{2,1,0:T(8,128)(2,1)S(1)}, u32[]{:S(2)}, u32[]{:S(2)}) async-start(bf16[8,16,3072]{2,1,0:T(8,128)(2,1)} %bitcast.4), calls=%async_computation.1 | async-start | bytes 1572864 | tf_op jit(solution)/shard_map/all_to_all | solution.py:28
  205.3 15.8 %all-to-all-start.2 = ((bf16[8,16,3072]{2,1,0:T(8,128)(2,1)}), bf16[8,16,3072]{2,1,0:T(8,128)(2,1)S(1)}, u32[]{:S(2)}, u32[]{:S(2)}) async-start(bf16[8,16,3072]{2,1,0:T(8,128)(2,1)} %broadcast_in_dim.9), calls=%async_computation.2 | async-start | bytes 1572864 | tf_op jit(solution)/shard_map/all_to_all | solution.py:34
  210.1 109.9 %all-gather.5.cloned.1.call-start = ((), (), s32[]{:S(2)}) async-start(), calls=%async_computation.10 | async-start | bytes 3538944 | tf_op jit(solution)/shard_map/all_gather | solution.py:13
  222.1 32.2 %all-to-all-start.5 = ((bf16[8,16,3072]{2,1,0:T(8,128)(2,1)}), bf16[8,16,3072]{2,1,0:T(8,128)(2,1)S(1)}, u32[]{:S(2)}, u32[]{:S(2)}) async-start(bf16[8,16,3072]{2,1,0:T(8,128)(2,1)} %broadcast_in_dim.10), calls=%async_computation.5 | async-start | bytes 1572864 | tf_op jit(solution)/shard_map/all_to_all | solution.py:34
  254.2 17.2 %all-to-all-start.3 = ((bf16[8,16,768]{2,1,0:T(8,128)(2,1)}), bf16[8,16,768]{2,1,0:T(8,128)(2,1)S(1)}, u32[]{:S(2)}, u32[]{:S(2)}) async-start(bf16[8,16,768]{2,1,0:T(8,128)(2,1)} %bitcast.6), calls=%async_computation.3 | async-start | bytes 393216 | tf_op jit(solution)/shard_map/all_to_all | solution.py:28
  271.5 13.1 %all-to-all-start.6 = ((bf16[8,16,768]{2,1,0:T(8,128)(2,1)}), bf16[8,16,768]{2,1,0:T(8,128)(2,1)S(1)}, u32[]{:S(2)}, u32[]{:S(2)}) async-start(bf16[8,16,768]{2,1,0:T(8,128)(2,1)} %bitcast.11), calls=%async_computation.6 | async-start | bytes 393216 | tf_op jit(solution)/shard_map/all_to_all | solution.py:28
  284.5 30.5 %all-to-all-start.7 = ((bf16[128,8,384]{2,0,1:T(8,128)(2,1)}), bf16[128,8,384]{2,0,1:T(8,128)(2,1)S(1)}, u32[]{:S(2)}, u32[]{:S(2)}) async-start(bf16[128,8,384]{2,0,1:T(8,128)(2,1)} %copy.14), calls=%async_computation.7 | async-start | bytes 1572864 | tf_op jit(solution)/shard_map/all_to_all | solution.py:112
  315.1 26.8 %all-to-all-start.8 = ((bf16[128,8,384]{2,0,1:T(8,128)(2,1)}), bf16[128,8,384]{2,0,1:T(8,128)(2,1)S(1)}, u32[]{:S(2)}, u32[]{:S(2)}) async-start(bf16[128,8,384]{2,0,1:T(8,128)(2,1)} %copy.15), calls=%async_computation.8 | async-start | bytes 1572864 | tf_op jit(solution)/shard_map/all_to_all | solution.py:113
Sparse Core Ops, SparseCore 0:
  10.1 120.8 all-gather.2
  213.0 51.8 all-gather.4
